TPU v7x, 32 devices: a whole 2x2x4 slice. The times are simulated.
32 devices in a mesh: group: 2 (over core), replica: 16 (over z, y, x).
Axes of the slice: x: 2, y: 2, z: 4, core: 2. Of those that a mesh axis runs over, the one named last changes fastest.
Arguments:
- latents: bfloat16 [16, 1024, 1024], P('replica', 'group'), may hold values from -6 to 6
- cond: bfloat16 [16, 1024], P('replica'), may hold values from -6 to 6
- cotangent: bfloat16 [16, 1024, 1024], P('replica', 'group'), may hold values from -6 to 6
- ada_weight: bfloat16 [1024, 6144], P('group'), may hold values from -0.1875 to 0.1875
- ada_bias: bfloat16 [6144], P('group'), may hold values from -4 to 4
- qkv_weight: bfloat16 [1024, 3072], P('group'), may hold values from -0.1875 to 0.1875
- query_bias: bfloat16 [1024], P('group'), may hold values from -4 to 4
- value_bias: bfloat16 [1024], P('group'), may hold values from -4 to 4
- output_weight: bfloat16 [1024, 1024], P('group'), may hold values from -0.75 to 0.75
- output_bias: bfloat16 [1024], P('group'), may hold values from -4 to 4
- up_weight: bfloat16 [1024, 4096], P('group'), may hold values from -0.1875 to 0.1875
- up_bias: bfloat16 [4096], P('group'), may hold values from -4 to 4
- down_weight: bfloat16 [4096, 1024], P('group'), may hold values from -0.09375 to 0.09375
- down_bias: bfloat16 [1024], P('group'), may hold values from -4 to 4
Outputs:
- block_out: bfloat16 [16, 1024, 1024], P('replica', 'group')
- latents_grad: float32 [16, 1024, 1024], P('replica', 'group')
- cond_grad: float32 [16, 1024], P('replica')
- ada_weight_grad: float32 [1024, 6144], P('group')
- ada_bias_grad: float32 [6144], P('group')
- qkv_weight_grad: float32 [1024, 3072], P('group')
- query_bias_grad: float32 [1024], P('group')
- value_bias_grad: float32 [1024], P('group')
- output_weight_grad: float32 [1024, 1024], P('group')
- output_bias_grad: float32 [1024], P('group')
- up_weight_grad: float32 [1024, 4096], P('group')
- up_bias_grad: float32 [4096], P('group')
- down_weight_grad: float32 [4096, 1024], P('group')
- down_bias_grad: float32 [1024], P('group')
All inputs are finite; a program needn't handle non-finite values.
Results may differ from a plain program's by a relative error of at most 0.02.
The roundings to bfloat16 on the way count: a program that leaves them out, or rounds other values in their place, can miss the bound.
Values may be sent and summed in bfloat16 or wider, within the bound.
A program may use at most 256 MiB of HBM per device.

v0:
```python
import jax
import jax.numpy as jnp
from jax import lax
from jax.sharding import PartitionSpec as P

HEADS = 16


def norm_rows(values):
    center = values - jnp.mean(values, axis=-1, keepdims=True)
    inverse = lax.rsqrt(jnp.mean(center * center, axis=-1, keepdims=True) + 1e-06)
    return (center * inverse, inverse)


def norm_back(normed, inverse, grad_normed):
    first = jnp.mean(grad_normed, axis=-1, keepdims=True)
    second = jnp.mean(grad_normed * normed, axis=-1, keepdims=True)
    return inverse * (grad_normed - first - normed * second)


def token_sum(values):
    return jnp.sum(values, axis=1)


def per_device(
    latents,
    cond,
    cotangent,
    ada_weight,
    ada_bias,
    qkv_weight,
    query_bias,
    value_bias,
    output_weight,
    output_bias,
    up_weight,
    up_bias,
    down_weight,
    down_bias,
):
    count_lat, local_len, width = latents.shape
    row_count = count_lat * local_len
    head_dim = width // HEADS
    factor = head_dim ** (-0.5)
    my_index = lax.axis_index("group")
    gathered = (
        lax.all_gather(qkv_weight, "group", axis=0, tiled=True),
        lax.all_gather(output_weight, "group", axis=0, tiled=True),
        lax.all_gather(up_weight, "group", axis=0, tiled=True),
        lax.all_gather(down_weight, "group", axis=0, tiled=True),
        lax.all_gather(query_bias, "group", axis=0, tiled=True),
        lax.all_gather(value_bias, "group", axis=0, tiled=True),
        lax.all_gather(output_bias, "group", axis=0, tiled=True),
        lax.all_gather(up_bias, "group", axis=0, tiled=True),
        lax.all_gather(down_bias, "group", axis=0, tiled=True),
        lax.all_gather(ada_bias, "group", axis=0, tiled=True),
    )
    (
        qkv_full,
        output_full,
        up_full,
        down_full,
        query_full,
        value_full,
        outbias_full,
        upbias_full,
        downbias_full,
        adabias_full,
    ) = gathered
    cond_float = cond.astype(jnp.float32)
    silu_cond, silu_back = jax.vjp(jax.nn.silu, cond_float)
    silu_low = silu_cond.astype(jnp.bfloat16)
    shard_rows = ada_weight.shape[0]
    silu_mine = lax.dynamic_slice_in_dim(silu_low, my_index * shard_rows, shard_rows, 1)
    partial_mod = jnp.dot(silu_mine, ada_weight, preferred_element_type=jnp.float32)
    modulation = lax.psum(partial_mod, "group") + adabias_full.astype(jnp.float32)
    parts = [modulation[:, None, index * width : (index + 1) * width] for index in range(6)]
    shift_one, scale_one, gate_one, shift_two, scale_two, gate_two = parts
    latent_float = latents.astype(jnp.float32)
    normed_one, inverse_one = norm_rows(latent_float)
    attn_in = (normed_one * (1.0 + scale_one) + shift_one).astype(jnp.bfloat16)
    attn_flat = attn_in.reshape(row_count, width)
    projected = jnp.dot(attn_flat, qkv_full, preferred_element_type=jnp.float32)
    queries = (
        (projected[:, :width] + query_full.astype(jnp.float32))
        .astype(jnp.bfloat16)
        .reshape(count_lat, local_len, width)
    )
    key_rows = (
        projected[:, width : 2 * width].astype(jnp.bfloat16).reshape(count_lat, local_len, width)
    )
    value_rows = (
        (projected[:, 2 * width :] + value_full.astype(jnp.float32))
        .astype(jnp.bfloat16)
        .reshape(count_lat, local_len, width)
    )
    key_whole, value_whole = (
        lax.all_gather(key_rows, "group", axis=1, tiled=True),
        lax.all_gather(value_rows, "group", axis=1, tiled=True),
    )

    def attend(items):
        query_part, key_part, value_part = items
        query_heads = query_part.reshape(local_len, HEADS, head_dim)
        key_heads = key_part.reshape(-1, HEADS, head_dim)
        value_heads = value_part.reshape(-1, HEADS, head_dim)
        scores = (
            jnp.einsum("qhd,khd->hqk", query_heads, key_heads, preferred_element_type=jnp.float32)
            * factor
        )
        top_score = jnp.max(scores, axis=-1, keepdims=True)
        expo = jnp.exp(scores - top_score)
        total = jnp.sum(expo, axis=-1, keepdims=True)
        weights_soft = (expo / total).astype(jnp.bfloat16)
        mixed_part = jnp.einsum(
            "hqk,khd->qhd", weights_soft, value_heads, preferred_element_type=jnp.float32
        )
        return (mixed_part.reshape(local_len, width), top_score + jnp.log(total))

    mixed, log_total = lax.map(attend, (queries, key_whole, value_whole))
    mixed_low = mixed.astype(jnp.bfloat16).reshape(row_count, width)
    branch_one = (
        jnp.dot(mixed_low, output_full, preferred_element_type=jnp.float32)
        + outbias_full.astype(jnp.float32)
    ).reshape(count_lat, local_len, width)
    middle = latent_float + gate_one * branch_one
    normed_two, inverse_two = norm_rows(middle)
    mlp_in = (
        (normed_two * (1.0 + scale_two) + shift_two).astype(jnp.bfloat16).reshape(row_count, width)
    )
    hidden = jnp.dot(mlp_in, up_full, preferred_element_type=jnp.float32) + upbias_full.astype(
        jnp.float32
    )
    active, gelu_back = jax.vjp(lambda values: jax.nn.gelu(values, approximate=True), hidden)
    active_low = active.astype(jnp.bfloat16)
    branch_two = (
        jnp.dot(active_low, down_full, preferred_element_type=jnp.float32)
        + downbias_full.astype(jnp.float32)
    ).reshape(count_lat, local_len, width)
    block_out = (middle + gate_two * branch_two).astype(jnp.bfloat16)
    qkv_back, output_back, up_back, down_back = (
        lax.all_gather(qkv_weight, "group", axis=0, tiled=True),
        lax.all_gather(output_weight, "group", axis=0, tiled=True),
        lax.all_gather(up_weight, "group", axis=0, tiled=True),
        lax.all_gather(down_weight, "group", axis=0, tiled=True),
    )
    grad_out = cotangent.astype(jnp.float32)
    grad_gate_two = token_sum(grad_out * branch_two)
    grad_branch_two = (grad_out * gate_two).reshape(row_count, width)
    down_bias_term = jnp.sum(grad_branch_two, axis=0)
    branch_two_low = grad_branch_two.astype(jnp.bfloat16)
    down_weight_term = jnp.dot(active_low.T, branch_two_low, preferred_element_type=jnp.float32)
    grad_active = jnp.dot(branch_two_low, down_back.T, preferred_element_type=jnp.float32).astype(
        jnp.bfloat16
    )
    grad_hidden = gelu_back(grad_active.astype(jnp.float32))[0]
    up_bias_term = jnp.sum(grad_hidden, axis=0)
    hidden_low = grad_hidden.astype(jnp.bfloat16)
    up_weight_term = jnp.dot(mlp_in.T, hidden_low, preferred_element_type=jnp.float32)
    grad_mlp_in = jnp.dot(hidden_low, up_back.T, preferred_element_type=jnp.float32).reshape(
        count_lat, local_len, width
    )
    grad_shift_two = token_sum(grad_mlp_in)
    grad_scale_two = token_sum(grad_mlp_in * normed_two)
    grad_middle = grad_out + norm_back(normed_two, inverse_two, grad_mlp_in * (1.0 + scale_two))
    grad_gate_one = token_sum(grad_middle * branch_one)
    grad_branch_one = (grad_middle * gate_one).reshape(row_count, width)
    output_bias_term = jnp.sum(grad_branch_one, axis=0)
    branch_one_low = grad_branch_one.astype(jnp.bfloat16)
    output_weight_term = jnp.dot(mixed_low.T, branch_one_low, preferred_element_type=jnp.float32)
    grad_mixed = (
        jnp.dot(branch_one_low, output_back.T, preferred_element_type=jnp.float32)
        .astype(jnp.bfloat16)
        .reshape(count_lat, local_len, width)
    )

    def attend_back(items):
        query_part, key_part, value_part, grad_part, log_part = items
        query_heads = query_part.reshape(local_len, HEADS, head_dim)
        key_heads = key_part.reshape(-1, HEADS, head_dim)
        value_heads = value_part.reshape(-1, HEADS, head_dim)
        grad_heads = grad_part.reshape(local_len, HEADS, head_dim)
        scores = (
            jnp.einsum("qhd,khd->hqk", query_heads, key_heads, preferred_element_type=jnp.float32)
            * factor
        )
        weights_soft = jnp.exp(scores - log_part)
        grad_soft = jnp.einsum(
            "qhd,khd->hqk", grad_heads, value_heads, preferred_element_type=jnp.float32
        )
        row_inner = jnp.sum(grad_soft * weights_soft, axis=-1, keepdims=True)
        grad_scores = (weights_soft * (grad_soft - row_inner)).astype(jnp.bfloat16)
        grad_query = (
            jnp.einsum("hqk,khd->qhd", grad_scores, key_heads, preferred_element_type=jnp.float32)
            * factor
        )
        grad_key = (
            jnp.einsum("hqk,qhd->khd", grad_scores, query_heads, preferred_element_type=jnp.float32)
            * factor
        )
        grad_value = jnp.einsum(
            "hqk,qhd->khd",
            weights_soft.astype(jnp.bfloat16),
            grad_heads,
            preferred_element_type=jnp.float32,
        )
        return (
            grad_query.reshape(local_len, width),
            grad_key.reshape(-1, width),
            grad_value.reshape(-1, width),
        )

    grad_query, key_terms, value_terms = lax.map(
        attend_back, (queries, key_whole, value_whole, grad_mixed, log_total)
    )
    grad_key, grad_value = (
        lax.psum_scatter(key_terms, "group", scatter_dimension=1, tiled=True),
        lax.psum_scatter(value_terms, "group", scatter_dimension=1, tiled=True),
    )
    query_low = grad_query.astype(jnp.bfloat16).reshape(row_count, width)
    key_low = grad_key.astype(jnp.bfloat16).reshape(row_count, width)
    value_low = grad_value.astype(jnp.bfloat16).reshape(row_count, width)
    query_bias_term = jnp.sum(query_low.astype(jnp.float32), axis=0)
    value_bias_term = jnp.sum(value_low.astype(jnp.float32), axis=0)
    grad_qkv = jnp.concatenate([query_low, key_low, value_low], axis=1)
    qkv_weight_term = jnp.dot(attn_flat.T, grad_qkv, preferred_element_type=jnp.float32)
    grad_attn_in = jnp.dot(grad_qkv, qkv_back.T, preferred_element_type=jnp.float32).reshape(
        count_lat, local_len, width
    )
    grad_shift_one = token_sum(grad_attn_in)
    grad_scale_one = token_sum(grad_attn_in * normed_one)
    latents_grad = grad_middle + norm_back(
        normed_one, inverse_one, grad_attn_in * (1.0 + scale_one)
    )
    mod_terms = jnp.concatenate(
        [
            grad_shift_one,
            grad_scale_one,
            grad_gate_one,
            grad_shift_two,
            grad_scale_two,
            grad_gate_two,
        ],
        axis=1,
    )
    grad_mod = lax.psum(mod_terms, "group")
    grad_mod_low = grad_mod.astype(jnp.bfloat16)
    bias_rows = ada_bias.shape[0]
    ada_bias_term = lax.dynamic_slice_in_dim(
        jnp.sum(grad_mod, axis=0), my_index * bias_rows, bias_rows, 0
    )
    ada_weight_term = jnp.dot(silu_mine.T, grad_mod_low, preferred_element_type=jnp.float32)
    silu_piece = jnp.dot(grad_mod_low, ada_weight.T, preferred_element_type=jnp.float32)
    silu_grad = lax.all_gather(silu_piece, "group", axis=1, tiled=True)
    cond_grad = silu_back(silu_grad)[0]
    shares = (
        lax.psum_scatter(
            qkv_weight_term.astype(jnp.bfloat16), "group", scatter_dimension=0, tiled=True
        ).astype(jnp.float32),
        lax.psum_scatter(
            output_weight_term.astype(jnp.bfloat16), "group", scatter_dimension=0, tiled=True
        ).astype(jnp.float32),
        lax.psum_scatter(
            up_weight_term.astype(jnp.bfloat16), "group", scatter_dimension=0, tiled=True
        ).astype(jnp.float32),
        lax.psum_scatter(
            down_weight_term.astype(jnp.bfloat16), "group", scatter_dimension=0, tiled=True
        ).astype(jnp.float32),
        lax.psum_scatter(
            query_bias_term.astype(jnp.bfloat16), "group", scatter_dimension=0, tiled=True
        ).astype(jnp.float32),
        lax.psum_scatter(
            value_bias_term.astype(jnp.bfloat16), "group", scatter_dimension=0, tiled=True
        ).astype(jnp.float32),
        lax.psum_scatter(
            output_bias_term.astype(jnp.bfloat16), "group", scatter_dimension=0, tiled=True
        ).astype(jnp.float32),
        lax.psum_scatter(
            up_bias_term.astype(jnp.bfloat16), "group", scatter_dimension=0, tiled=True
        ).astype(jnp.float32),
        lax.psum_scatter(
            down_bias_term.astype(jnp.bfloat16), "group", scatter_dimension=0, tiled=True
        ).astype(jnp.float32),
    )
    (
        qkv_share,
        output_share,
        up_share,
        down_share,
        query_share,
        value_share,
        outbias_share,
        upbias_share,
        downbias_share,
    ) = shares
    summed = (
        lax.psum(ada_weight_term.astype(jnp.bfloat16), "replica").astype(jnp.float32),
        lax.psum(ada_bias_term.astype(jnp.bfloat16), "replica").astype(jnp.float32),
        lax.psum(qkv_share.astype(jnp.bfloat16), "replica").astype(jnp.float32),
        lax.psum(query_share.astype(jnp.bfloat16), "replica").astype(jnp.float32),
        lax.psum(value_share.astype(jnp.bfloat16), "replica").astype(jnp.float32),
        lax.psum(output_share.astype(jnp.bfloat16), "replica").astype(jnp.float32),
        lax.psum(outbias_share.astype(jnp.bfloat16), "replica").astype(jnp.float32),
        lax.psum(up_share.astype(jnp.bfloat16), "replica").astype(jnp.float32),
        lax.psum(upbias_share.astype(jnp.bfloat16), "replica").astype(jnp.float32),
        lax.psum(down_share.astype(jnp.bfloat16), "replica").astype(jnp.float32),
        lax.psum(downbias_share.astype(jnp.bfloat16), "replica").astype(jnp.float32),
    )
    return (
        block_out,
        latents_grad,
        cond_grad,
        summed[0],
        summed[1],
        summed[2],
        summed[3],
        summed[4],
        summed[5],
        summed[6],
        summed[7],
        summed[8],
        summed[9],
        summed[10],
    )


def solution(mesh):
    return jax.shard_map(
        per_device,
        mesh=mesh,
        in_specs=(
            P("replica", "group", None),
            P("replica", None),
            P("replica", "group", None),
            P("group", None),
            P("group"),
            P("group", None),
            P("group"),
            P("group"),
            P("group", None),
            P("group"),
            P("group", None),
            P("group"),
            P("group", None),
            P("group"),
        ),
        out_specs=(
            P("replica", "group", None),
            P("replica", "group", None),
            P("replica", None),
            P("group", None),
            P("group"),
            P("group", None),
            P("group"),
            P("group"),
            P("group", None),
            P("group"),
            P("group", None),
            P("group"),
            P("group", None),
            P("group"),
        ),
        check_vma=False,
    )
```

profile of v0, /device:TPU:0, one launch (start us, length us, event | category | flops | bytes accessed | tf_op | source)
XLA Modules:
  0.0 882.2 jit_solution(9799312302023419380)
XLA Ops:
  12.1 3.7 fusion.58
  15.8 3.6 psum.91
  20.1 8.9 %all-gather.15.cloned.1.call-done = bf16[1024,3072]{1,0:T(8,128)(2,1)} async-done(((bf16[512,3072]{1,0:T(8,128)(2,1)}), bf16[1024,3072]{1,0:T(8,128)(2,1)}) %all-gather.15.cloned.1.call-update) | async-done | bytes 6291472 | tf_op jit(solution)/shard_map/all_gather | solution.py:47
  29.1 5.8 fusion.65
  42.4 3.8 fusion.33
  57.5 13.8 %multiply_reduce_fusion.1 = (f32[16,512]{1,0:T(8,128)S(1)}, f32[16,512,1024]{2,1,0:T(8,128)}) fusion(bf16[512,16,64]{0,2,1:T(8,128)(2,1)S(1)} %bitcast.129, bf16[1024,16,64]{0,2,1:T(8,128)(2,1)S(1)} %bitcast.126), kind=kOutput, calls=%fused_computation.6 | convolution fusion | flops 1090510848 | bytes 36732928 | tf_op jit(solution)/shard_map/while/body/eval_jaxpr/qhd,khd->hqk/dot_general | solution.py:108
  74.2 15.3 %fusion = f32[16,512]{1,0:T(8,128)S(1)} fusion(f32[16,512,1024]{2,1,0:T(8,128)} %get-tuple-element.105, f32[16,512]{1,0:T(8,128)S(1)} %get-tuple-element.104), kind=kLoop, calls=%fused_computation.5 | loop fusion | flops 25157632 | bytes 33619968 | tf_op jit(solution)/shard_map/while/body/eval_jaxpr/reduce_sum | solution.py:113
  89.5 16.7 %fusion.43 = bf16[16,64,512]{2,1,0:T(8,128)(2,1)} fusion(bf16[1024,16,64]{0,2,1:T(8,128)(2,1)S(1)} %bitcast.132, f32[16,512,1024]{2,1,0:T(8,128)} %get-tuple-element.105, f32[16,512]{1,0:T(8,128)S(1)} %fusion, f32[16,512]{1,0:T(8,128)S(1)} %get-tuple-element.104), kind=kOutput, calls=%fused_computation.84 | convolution fusion | flops 1107820544 | bytes 36765696 | tf_op jit(solution)/shard_map/while/body/eval_jaxpr/hqk,khd->qhd/dot_general | solution.py:115
  106.3 4.6 fusion.75
  112.6 13.8 %fusion.68 = f32[512,4096]{1,0:T(8,128)} fusion(bf16[1024,4096]{1,0:T(8,128)(2,1)} %all-gather.19.cloned.1.call-done, f32[1,512,1024]{2,1,0:T(8,128)} %copy-done.14, f32[1024]{0:T(1024)S(1)} %bitcast.156, f32[1024]{0:T(1024)S(1)} %bitcast.144, f32[512]{0:T(512)S(1)} %add_rsqrt_fusion, f32[512]{0:T(512)S(1)} %broadcast_multiply_fusion.4), kind=kOutput, calls=%fused_computation.128 | convolution fusion | flops 4297588736 | bytes 18886656 | tf_op jit(solution)/shard_map/dot_general | solution.py:131
  126.5 16.4 %fusion.78 = (bf16[4096]{0:T(1024)(128)(2,1)}, bf16[512,4096]{1,0:T(8,128)(2,1)}) fusion(f32[512,4096]{1,0:T(8,128)} %fusion.68, f32[4096]{0:T(1024)S(1)} %convert_element_type.220, bf16[4096,1024]{1,0:T(8,128)(2,1)} %all-gather.21.cloned.1.call-done, bf16[1,512,1024]{2,1,0:T(8,128)(2,1)S(1)} %copy-done.39, f32[1024]{0:T(1024)S(1)} %bitcast.158), kind=kOutput, calls=%fused_computation.136 | convolution fusion | flops 4346867712 | bytes 22048768 | tf_op jit(solution)/shard_map/dot_general | solution.py:153
  142.9 9.4 %fusion.35 = (f32[1024]{0:T(1024)}, f32[512]{0:T(512)S(1)}, f32[512,1024]{1,0:T(8,128)S(1)}) fusion(f32[1,512,1024]{2,1,0:T(8,128)S(1)} %copy-done.15, f32[512]{0:T(512)S(1)} %add_rsqrt_fusion, f32[512]{0:T(512)S(1)} %broadcast_multiply_fusion.4, f32[1024]{0:T(1024)S(1)} %bitcast.145, bf16[1024,4096]{1,0:T(8,128)(2,1)} %all-gather.19.cloned.1.call-done, ...), kind=kOutput, calls=%fused_computation.62 | convolution fusion | flops 4298635776 | bytes 16791552 | tf_op jit(solution)/shard_map/dot_general | solution.py:160
  152.6 10.3 %fusion.22 = (bf16[1024]{0:T(1024)(128)(2,1)S(1)}, f32[1024]{0:T(1024)S(1)}, bf16[1,512,1024]{2,1,0:T(8,128)(2,1)}, f32[1024]{0:T(1024)S(1)}, bf16[1024]{0:T(1024)(128)(2,1)S(1)}, /*index=5*/f32[1,512,1024]{2,1,0:T(8,128)S(1)}) fusion(bf16[1,512,1024]{2,1,0:T(8,128)(2,1)S(1)} %copy-done.39, f32[1024]{0:T(1024)S(1)} %bitcast.159, f32[1024]{0:T(1024)S(1)} %bitcast.170, ...), kind=kOutput, calls=%fused_computation.44 | convolution fusion | flops 4327469056 | bytes 27320320 | tf_op jit(solution)/shard_map/dot_general | solution.py:137
  168.0 15.7 %fusion.2 = f32[16,64,1024]{2,1,0:T(8,128)} fusion(bf16[512,16,64]{0,2,1:T(8,128)(2,1)S(1)} %bitcast.134, f32[16,512,1024]{2,1,0:T(8,128)} %get-tuple-element.105, f32[16,512]{1,0:T(8,128)S(1)} %log_add_fusion), kind=kOutput, calls=%fused_computation.8 | convolution fusion | flops 1098907648 | bytes 38830080 | tf_op jit(solution)/shard_map/while/body/eval_jaxpr/hqk,qhd->khd/dot_general | solution.py:201
  183.8 23.1 %multiply_reduce_fusion = (f32[16,512]{1,0:T(8,128)S(1)}, f32[16,512,1024]{2,1,0:T(8,128)}) fusion(f32[16,512,1024]{2,1,0:T(8,128)} %get-tuple-element.105, f32[16,512]{1,0:T(8,128)S(1)} %log_add_fusion, bf16[512,16,64]{0,2,1:T(8,128)(2,1)S(1)} %bitcast.135, bf16[1024,16,64]{0,2,1:T(8,128)(2,1)S(1)} %bitcast.133), kind=kOutput, calls=%fused_computation.1 | convolution fusion | flops 1107288064 | bytes 70320128 | tf_op jit(solution)/shard_map/while/body/eval_jaxpr/qhd,khd->hqk/dot_general | solution.py:188
  206.8 27.9 %multiply_convert_fusion = bf16[16,512,1024]{2,1,0:T(8,128)(2,1)} fusion(f32[16,512,1024]{2,1,0:T(8,128)} %get-tuple-element.109, f32[16,512,1024]{2,1,0:T(8,128)} %get-tuple-element.105, f32[16,512]{1,0:T(8,128)S(1)} %get-tuple-element.108, f32[16,512]{1,0:T(8,128)S(1)} %log_add_fusion), kind=kLoop, calls=%fused_computation | loop fusion | flops 41943040 | bytes 83951616 | tf_op jit(solution)/shard_map/while/body/eval_jaxpr/convert_element_type | solution.py:192
  234.8 10.7 %convolution_multiply_fusion = f32[16,64,1024]{2,1,0:T(8,128)} fusion(bf16[512,16,64]{0,2,1:T(8,128)(2,1)S(1)} %bitcast.130, bf16[16,512,1024]{2,1,0:T(8,128)(2,1)} %multiply_convert_fusion), kind=kOutput, calls=%fused_computation.46 | convolution fusion | flops 1074790400 | bytes 22020096 | tf_op jit(solution)/shard_map/while/body/eval_jaxpr/hqk,qhd->khd/dot_general | solution.py:198
  247.1 3.8 convolution_convert_fusion.4
  251.1 14.3 %convolution_convert_fusion = bf16[4096,1024]{1,0:T(8,128)(2,1)} fusion(bf16[1,512,1024]{2,1,0:T(8,128)(2,1)S(1)} %copy-done.40, f32[1024]{0:T(1024)S(1)} %bitcast.160, f32[512,4096]{1,0:T(8,128)} %fusion.68, f32[4096]{0:T(1024)S(1)} %convert_element_type.220), kind=kOutput, calls=%fused_computation.27 | convolution fusion | flops 4321705984 | bytes 17846272 | tf_op jit(solution)/shard_map/dot_general | solution.py:152
  267.1 9.9 %convolution_convert_fusion.1 = bf16[1024,4096]{1,0:T(8,128)(2,1)} fusion(bf16[512,4096]{1,0:T(8,128)(2,1)} %get-tuple-element.114, f32[1,512,1024]{2,1,0:T(8,128)S(1)} %copy-done.16, f32[1024]{0:T(1024)S(1)} %bitcast.157, f32[1024]{0:T(1024)S(1)} %bitcast.148, f32[512]{0:T(512)S(1)} %add_rsqrt_fusion, f32[512]{0:T(512)S(1)} %broadcast_multiply_fusion.4), kind=kOutput, calls=%fused_computation.28 | convolution fusion | flops 4301783040 | bytes 14692352 | tf_op jit(solution)/shard_map/dot_general | solution.py:159
  278.6 13.0 %fusion.77 = (bf16[16,64]{1,0:T(8,128)(2,1)S(1)}, bf16[16,64,512]{2,1,0:T(8,128)(2,1)}) fusion(bf16[1024,16,64]{0,2,1:T(8,128)(2,1)S(1)} %bitcast.127, bf16[16,512,1024]{2,1,0:T(8,128)(2,1)} %multiply_convert_fusion), kind=kOutput, calls=%fused_computation.135 | convolution fusion | flops 1075313664 | bytes 19924992 | tf_op jit(solution)/shard_map/while/body/eval_jaxpr/hqk,khd->qhd/dot_general | solution.py:194
  295.4 7.7 convolution_convert_fusion.3
  303.8 8.4 fusion.30
  313.9 4.2 psum.92
  318.2 4.1 multiply_convert_fusion.1
  322.2 10.3 %reduce-scatter.11.cloned.1.call-done = bf16[512,3072]{1,0:T(8,128)(2,1)} async-done(((bf16[1024,3072]{1,0:T(8,128)(2,1)}), bf16[512,3072]{1,0:T(8,128)(2,1)}) %reduce-scatter.11.cloned.1.call-update) | async-done | bytes 3145744 | tf_op jit(solution)/shard_map/reduce_scatter | solution.py:257
  339.3 81.4 %all-reduce.5 = (bf16[3072]{0:T(1024)(128)(2,1)S(1)}, bf16[512]{0:T(512)(128)(2,1)S(1)}, bf16[512]{0:T(512)(128)(2,1)S(1)}, bf16[512]{0:T(512)(128)(2,1)S(1)}, b...) all-reduce(bf16[3072]{0:T(1024)(128)(2,1)S(1)} %convert_reduce_fusi, ...), channel_id=1, replica_groups=mesh['group'=2,'replica'=16] {'replica'}, use_global_device_ids=true, to_apply=%region_22.23 | all-reduce | flops 7168 | bytes 28672 | tf_op jit(solution)/shard_map/psum | solution.py:298
  424.2 4.8 convolution_bitcast_fusion
  433.8 417.0 %all-reduce.10.cloned.1.call-done = (bf16[512,6144]{1,0:T(8,128)(2,1)}, bf16[512,3072]{1,0:T(8,128)(2,1)}, bf16[512,1024]{1,0:T(8,128)(2,1)}, bf16[512,4096]{1,0:T(8,128)(2,1)}, bf16[2048,1024]{1,0:T(8,128)(2,1)}) async-done(((bf16[512,6144]{1,0:T(8,128)(2,1)}, bf16[512,3072]{1,0:T(8,128)(2,1)}, bf16[512,1024]{1,0:T(8,128)(2,1)}, bf16[512,4096]{1,0:T(8,128)(2,1)}, bf16[2048,1024]{1,0:T(8,128)(2,1)}), ...) | async-done | bytes 18874384 | tf_op jit(solution)/shard_map/psum | solution.py:297
  853.5 9.4 %convert_element_type.242 = f32[512,6144]{1,0:T(8,128)} convert(bf16[512,6144]{1,0:T(8,128)(2,1)} %get-tuple-element.77) | non-fusion elementwise | flops 3145728 | bytes 18874368 | tf_op jit(solution)/shard_map/convert_element_type | solution.py:297
  866.4 4.5 convert_element_type.255
  870.9 4.4 convert_element_type.259
  (194 shorter events, 65.3 us)
Async XLA Ops:
  7.2 12.2 %copy-start.4 = (bf16[1,512,1024]{2,1,0:T(8,128)(2,1)S(1)}, bf16[1,512,1024]{2,1,0:T(8,128)(2,1)}, u32[]{:S(2)}) copy-start(bf16[1,512,1024]{2,1,0:T(8,128)(2,1)} %param.14) | copy-start | bytes 3145732
  7.2 21.9 %all-gather.15.cloned.1.call-start = ((), (), s32[]{:S(2)}) async-start(), calls=%async_computation.6 | async-start | bytes 9437184 | tf_op jit(solution)/shard_map/all_gather | solution.py:47
  7.9 46.3 %all-gather.25.cloned.1.call-start = ((), (), s32[]{:S(2)}) async-start(), calls=%async_computation.17 | async-start | bytes 3145728 | tf_op jit(solution)/shard_map/all_gather | solution.py:98
  19.7 15.2 %copy-start.23 = (f32[512]{0:T(512)}, f32[512]{0:T(512)S(1)}, u32[]{:S(2)}) copy-start(f32[512]{0:T(512)S(1)} %broadcast_multiply_fusion.5) | copy-start | bytes 6148
  20.1 14.8 %copy-start.26 = (f32[512]{0:T(512)}, f32[512]{0:T(512)S(1)}, u32[]{:S(2)}) copy-start(f32[512]{0:T(512)S(1)} %add_rsqrt_fusion.1) | copy-start | bytes 6148
  20.1 14.8 %copy-start.20 = (f32[1,1024]{1,0:T(1,128)}, f32[1,1024]{1,0:T(1,128)S(1)}, u32[]{:S(2)}) copy-start(f32[1,1024]{1,0:T(1,128)S(1)} %get-tuple-element.102) | copy-start | bytes 12292
  20.1 14.8 %copy-start.29 = (f32[1,1024]{1,0:T(1,128)}, f32[1,1024]{1,0:T(1,128)S(1)}, u32[]{:S(2)}) copy-start(f32[1,1024]{1,0:T(1,128)S(1)} %get-tuple-element.101) | copy-start | bytes 12292
  29.1 9.7 %copy-start.33 = (bf16[512]{0:T(512)(128)(2,1)S(1)}, bf16[512]{0:T(512)(128)(2,1)}, u32[]{:S(2)}) copy-start(bf16[512]{0:T(512)(128)(2,1)} %param.20) | copy-start | bytes 3076
  29.1 11.6 %copy-start.34 = (bf16[512]{0:T(512)(128)(2,1)S(1)}, bf16[512]{0:T(512)(128)(2,1)}, u32[]{:S(2)}) copy-start(bf16[512]{0:T(512)(128)(2,1)} %param.21) | copy-start | bytes 3076
  38.8 32.5 %all-gather.23.cloned.1.call-start = ((), (), s32[]{:S(2)}) async-start(), calls=%async_computation.16 | async-start | bytes 3145728 | tf_op jit(solution)/shard_map/all_gather | solution.py:99
  46.2 60.0 %all-gather.17.cloned.1.call-start = ((), (), s32[]{:S(2)}) async-start(), calls=%async_computation.7 | async-start | bytes 3145728 | tf_op jit(solution)/shard_map/all_gather | solution.py:48
  46.9 65.8 %all-gather.19.cloned.1.call-start = ((), (), s32[]{:S(2)}) async-start(), calls=%async_computation.8 | async-start | bytes 12582912 | tf_op jit(solution)/shard_map/all_gather | solution.py:49
  47.4 79.0 %all-gather.21.cloned.1.call-start = ((), (), s32[]{:S(2)}) async-start(), calls=%async_computation.9 | async-start | bytes 12582912 | tf_op jit(solution)/shard_map/all_gather | solution.py:50
  48.0 243.6 %reduce-scatter.9.cloned.1.call-start = ((), (), s32[]{:S(2)}) async-start(), calls=%async_computation.11 | async-start | bytes 6291456 | tf_op jit(solution)/shard_map/reduce_scatter | solution.py:218
  54.2 17.1 %copy-start.2 = (bf16[512,1024]{0,1:T(8,128)(2,1)}, bf16[512,1024]{0,1:T(8,128)(2,1)S(1)}, u32[]{:S(2)}) copy-start(bf16[512,1024]{0,1:T(8,128)(2,1)S(1)} %copy.41) | copy-start | bytes 3145732
  57.5 13.8 %copy-start = (bf16[1024,1024]{0,1:T(8,128)(2,1)}, bf16[1024,1024]{0,1:T(8,128)(2,1)S(1)}, u32[]{:S(2)}) copy-start(bf16[1024,1024]{0,1:T(8,128)(2,1)S(1)} %copy.42) | copy-start | bytes 6291460
  89.5 16.8 %copy-start.5 = (bf16[1,512,1024]{2,1,0:T(8,128)(2,1)S(1)}, bf16[1,512,1024]{2,1,0:T(8,128)(2,1)}, u32[]{:S(2)}) copy-start(bf16[1,512,1024]{2,1,0:T(8,128)(2,1)} %param.14) | copy-start | bytes 3145732
  112.6 13.9 %copy-start.39 = (bf16[1,512,1024]{2,1,0:T(8,128)(2,1)S(1)}, bf16[1,512,1024]{2,1,0:T(8,128)(2,1)}, u32[]{:S(2)}) copy-start(bf16[1,512,1024]{2,1,0:T(8,128)(2,1)} %param.16) | copy-start | bytes 3145732
  126.5 16.4 %copy-start.15 = (f32[1,512,1024]{2,1,0:T(8,128)S(1)}, f32[1,512,1024]{2,1,0:T(8,128)}, u32[]{:S(2)}) copy-start(f32[1,512,1024]{2,1,0:T(8,128)} %copy-done.14) | copy-start | bytes 6291460
  142.9 9.7 %copy-start.42 = (f32[512,1024]{1,0:T(8,128)S(1)}, f32[512,1024]{1,0:T(8,128)}, u32[]{:S(2)}) copy-start(f32[512,1024]{1,0:T(8,128)} %get-tuple-element.106) | copy-start | bytes 6291460
  152.6 11.6 %copy-start.38 = (bf16[1024,1024]{1,0:T(8,128)(2,1)S(1)}, bf16[1024,1024]{1,0:T(8,128)(2,1)}, u32[]{:S(2)}) copy-start(bf16[1024,1024]{1,0:T(8,128)(2,1)} %all-gather.17.cloned.1.call-done) | copy-start | bytes 6291460
  183.7 109.9 %reduce-scatter.7.cloned.1.call-start = ((), (), s32[]{:S(2)}) async-start(), calls=%async_computation.10 | async-start | bytes 6291456 | tf_op jit(solution)/shard_map/reduce_scatter | solution.py:217
  206.8 27.9 %copy-start.3 = (bf16[512,1024]{0,1:T(8,128)(2,1)S(1)}, bf16[512,1024]{0,1:T(8,128)(2,1)}, u32[]{:S(2)}) copy-start(bf16[512,1024]{0,1:T(8,128)(2,1)} %copy-done.2) | copy-start | bytes 3145732
  245.5 76.7 %reduce-scatter.13.cloned.1.call-start = ((), (), s32[]{:S(2)}) async-start(), calls=%async_computation.13 | async-start | bytes 3145728 | tf_op jit(solution)/shard_map/reduce_scatter | solution.py:260
  250.9 71.3 %reduce-scatter.17.cloned.1.call-start = ((), (), s32[]{:S(2)}) async-start(), calls=%async_computation.15 | async-start | bytes 12582912 | tf_op jit(solution)/shard_map/reduce_scatter | solution.py:266
  265.5 56.7 %reduce-scatter.15.cloned.1.call-start = ((), (), s32[]{:S(2)}) async-start(), calls=%async_computation.14 | async-start | bytes 12582912 | tf_op jit(solution)/shard_map/reduce_scatter | solution.py:263
  277.0 55.6 %reduce-scatter.11.cloned.1.call-start = ((), (), s32[]{:S(2)}) async-start(), calls=%async_computation.12 | async-start | bytes 9437184 | tf_op jit(solution)/shard_map/reduce_scatter | solution.py:257
  303.2 547.6 %all-reduce.10.cloned.1.call-start = ((), (), s32[]{:S(2)}) async-start(), calls=%async_computation.18 | async-start | bytes 37748736 | tf_op jit(solution)/shard_map/psum | solution.py:297
  303.8 10.0 %copy-start.32 = (f32[1024]{0:T(1024)S(1)}, f32[1024]{0:T(1024)}, u32[]{:S(2)}) copy-start(f32[1024]{0:T(1024)} %get-tuple-element.50) | copy-start | bytes 12292
  335.2 95.9 %copy-start.22 = (bf16[1,1024]{1,0:T(2,128)(2,1)S(1)}, bf16[1,1024]{1,0:T(2,128)(2,1)}, u32[]{:S(2)}) copy-start(bf16[1,1024]{1,0:T(2,128)(2,1)} %param.15) | copy-start | bytes 6148
  335.4 96.4 %copy-start.9 = (f32[512,1024]{1,0:T(8,128)S(1)}, f32[512,1024]{1,0:T(8,128)}, u32[]{:S(2)}) copy-start(f32[512,1024]{1,0:T(8,128)} %copy-done.8) | copy-start | bytes 6291460
  420.7 11.1 %copy-start.19 = (f32[1,512,1024]{2,1,0:T(8,128)S(1)}, f32[1,512,1024]{2,1,0:T(8,128)}, u32[]{:S(2)}) copy-start(f32[1,512,1024]{2,1,0:T(8,128)} %copy-done.17) | copy-start | bytes 6291460
  (24 other events, 78.9 us)
Sparse Core Ops, SparseCore 0:
  9.6 19.4 all-gather.14
  38.9 11.7 all-gather.24
  52.8 11.7 all-gather.22
  66.0 11.7 all-gather.16
  79.1 21.0 all-gather.18
  101.6 21.0 all-gather.20
  183.8 13.2 reduce-scatter.8
  245.6 13.2 reduce-scatter.6
  261.2 10.8 reduce-scatter.12
  274.9 17.9 reduce-scatter.16
  295.8 18.0 reduce-scatter.14
  316.7 15.7 reduce-scatter.10
  339.6 511.1 all-reduce.9
where the time goes:
time: 887 us; the launch traced here: 882 us
  waiting for transfers between devices  439 us (49%)
  matrix products  208 us (23%)
  blocking collectives  106 us (12%)
  other arithmetic  89.4 us (10%)
  local copies, waits for them, and re-layouts  22.6 us (3%)
  between operations  16.1 us (2%)
    psum x1, waiting for transfers between devices, per_device(): lax.psum(ada_weight_term.astype(jnp.bfloat16), 'replica')  417 us
    psum x1, blocking collectives, per_device(): lax.psum(ada_bias_term.astype(jnp.bfloat16), 'replica').astype(jnp.float32)  81.4 us
    convert_element_type x1, other arithmetic, attend_back(): grad_scores = (weights_soft * (grad_soft - row_inner)).astype(jnp.bfloat16)  27.9 us
    dot_general x1, matrix products, attend_back(): jnp.einsum('qhd,khd->hqk', grad_heads, value_heads, preferred_element_typ...  23.1 us
  transfers between devices with their start and end apart: 13, of which 3 were waited for; matrix products, arithmetic and copies ran while one was open for 25% of the time, Pallas kernels for 0%

commit v1 on v0

v1 whole, which is shorter than its diff:
```python
import functools

import jax
import jax.numpy as jnp
from jax import lax
from jax.experimental import pallas as pl
from jax.experimental.pallas import tpu as pltpu
from jax.sharding import PartitionSpec as P

HEADS = 16


def norm_rows(values):
    center = values - jnp.mean(values, axis=-1, keepdims=True)
    inverse = lax.rsqrt(jnp.mean(center * center, axis=-1, keepdims=True) + 1e-06)
    return (center * inverse, inverse)


def norm_back(normed, inverse, grad_normed):
    first = jnp.mean(grad_normed, axis=-1, keepdims=True)
    second = jnp.mean(grad_normed * normed, axis=-1, keepdims=True)
    return inverse * (grad_normed - first - normed * second)


def token_sum(values):
    return jnp.sum(values, axis=1)


def head_masks(width, head_dim, dtype):
    lane = lax.broadcasted_iota(jnp.int32, (1, width), 1)
    return [
        jnp.where((lane >= first) & (lane < first + head_dim), 1.0, 0.0).astype(dtype)
        for first in range(0, width, head_dim)
    ]


def contract(left, right, left_dim, right_dim):
    return lax.dot_general(
        left,
        right,
        (((left_dim,), (right_dim,)), ((), ())),
        preferred_element_type=jnp.float32,
    )


def attend_kernel(head_dim, query_ref, key_ref, value_ref, mixed_ref):
    factor = head_dim ** (-0.5)
    key_part, value_part = key_ref[...], value_ref[...]
    masks = head_masks(key_part.shape[1], head_dim, jnp.bfloat16)
    total_mixed = None
    for mask in masks:
        query_part = query_ref[...] * (mask * factor).astype(jnp.bfloat16)
        scores = contract(query_part, key_part, 1, 1)
        expo = jnp.exp(scores - jnp.max(scores, axis=-1, keepdims=True))
        share = 1.0 / jnp.sum(expo, axis=-1, keepdims=True)
        weights_soft = (expo * share).astype(jnp.bfloat16)
        mixed = contract(weights_soft, value_part * mask, 1, 0)
        total_mixed = mixed if total_mixed is None else total_mixed + mixed
    mixed_ref[...] = total_mixed.astype(mixed_ref.dtype)


def attend_back_kernel(
    head_dim, query_ref, key_ref, value_ref, grad_ref, query_grad_ref, key_grad_ref, value_grad_ref
):
    factor = head_dim ** (-0.5)
    key_part, value_part = key_ref[...], value_ref[...]
    masks = head_masks(key_part.shape[1], head_dim, jnp.bfloat16)
    query_grad = key_grad = value_grad = 0.0
    for mask in masks:
        query_part = query_ref[...] * (mask * factor).astype(jnp.bfloat16)
        grad_part = grad_ref[...] * mask
        scores = contract(key_part, query_part, 1, 1)
        expo = jnp.exp(scores - jnp.max(scores, axis=0, keepdims=True))
        weights_soft = expo * (1.0 / jnp.sum(expo, axis=0, keepdims=True))
        grad_soft = contract(value_part, grad_part, 1, 1)
        inner = jnp.sum(grad_soft * weights_soft, axis=0, keepdims=True)
        grad_scores = (weights_soft * (grad_soft - inner)).astype(jnp.bfloat16)
        value_grad += contract(weights_soft.astype(jnp.bfloat16), grad_part, 1, 0)
        key_grad += contract(grad_scores, query_part, 1, 0)
        query_grad += contract(key_part * mask, grad_scores, 0, 0)
    query_grad_ref[...] = (jnp.transpose(query_grad) * factor).astype(query_grad_ref.dtype)
    key_grad_ref[...] = key_grad
    value_grad_ref[...] = value_grad


def attention(queries, keys, values, head_dim):
    rows, width = queries.shape
    length = keys.shape[0]
    block = max(128, head_dim)
    short = pl.BlockSpec((rows, block), lambda index: (0, index))
    tall = pl.BlockSpec((length, block), lambda index: (0, index))
    return pl.pallas_call(
        functools.partial(attend_kernel, head_dim),
        grid=(width // block,),
        in_specs=[short, tall, tall],
        out_specs=short,
        out_shape=jax.ShapeDtypeStruct((rows, width), jnp.bfloat16),
        compiler_params=pltpu.CompilerParams(vmem_limit_bytes=48 * 2**20),
        cost_estimate=pl.CostEstimate(
            flops=16 * rows * length * width,
            bytes_accessed=4 * (rows + length) * width,
            transcendentals=rows * length * (width // head_dim),
        ),
        name="attend",
    )(queries, keys, values)


def attention_back(queries, keys, values, grads, head_dim):
    rows, width = queries.shape
    length = keys.shape[0]
    block = max(128, head_dim)
    short = pl.BlockSpec((rows, block), lambda index: (0, index))
    tall = pl.BlockSpec((length, block), lambda index: (0, index))
    return pl.pallas_call(
        functools.partial(attend_back_kernel, head_dim),
        grid=(width // block,),
        in_specs=[short, tall, tall, short],
        out_specs=[short, tall, tall],
        out_shape=[
            jax.ShapeDtypeStruct((rows, width), jnp.bfloat16),
            jax.ShapeDtypeStruct((length, width), jnp.float32),
            jax.ShapeDtypeStruct((length, width), jnp.float32),
        ],
        compiler_params=pltpu.CompilerParams(vmem_limit_bytes=48 * 2**20),
        cost_estimate=pl.CostEstimate(
            flops=40 * rows * length * width,
            bytes_accessed=8 * (rows + 2 * length) * width,
            transcendentals=rows * length * (width // head_dim),
        ),
        name="attend_back",
    )(queries, keys, values, grads)


def turn(values, axis, shift):
    count = lax.axis_size(axis)
    return lax.ppermute(values, axis, [(at, (at + shift) % count) for at in range(count)])


def group_rows(left, right, rows):
    count, place = lax.axis_size("group"), lax.axis_index("group")

    def term(owner):
        part = lax.dynamic_slice_in_dim(left, owner * rows, rows, 1)
        return jnp.dot(part.T, right, preferred_element_type=jnp.float32)

    away = [
        turn(term((place + shift) % count).astype(jnp.bfloat16), "group", shift)
        for shift in range(1, count)
    ]
    total = term(place)
    for item in away:
        total = total + item.astype(jnp.float32)
    return total.astype(jnp.bfloat16)


def pair_sum(values, bits):
    place = lax.axis_index("replica")
    pairs = [[(at, at ^ bit) for at in range(lax.axis_size("replica"))] for bit in bits]
    for bit, pair in zip(bits, pairs):
        half = values.shape[0] // 2
        upper = (place & bit) != 0
        low, high = values[:half], values[half:]
        away = lax.ppermute(jnp.where(upper, low, high), "replica", pair)
        values = jnp.where(upper, high, low) + away
    for bit, pair in reversed(list(zip(bits, pairs))):
        upper = (place & bit) != 0
        away = lax.ppermute(values, "replica", pair)
        values = jnp.where(
            upper, jnp.concatenate([away, values]), jnp.concatenate([values, away])
        )
    return values


def replica_sum(values):
    count, rows = lax.axis_size("replica"), values.shape[0]
    if count & (count - 1) or rows % count:
        return lax.psum(values, "replica")
    bits = [1 << step for step in range(count.bit_length() - 1)]
    cut = (values.shape[1] // 256) * 128
    first = pair_sum(values[:, :cut], bits)
    second = pair_sum(values[:, cut:], bits[1:2] + bits[:1] + bits[2:])
    return jnp.concatenate([first, second], axis=1)


def after(values, earlier):
    return lax.optimization_barrier((values, earlier))[0]


def per_device(
    latents,
    cond,
    cotangent,
    ada_weight,
    ada_bias,
    qkv_weight,
    query_bias,
    value_bias,
    output_weight,
    output_bias,
    up_weight,
    up_bias,
    down_weight,
    down_bias,
):
    count_lat, local_len, width = latents.shape
    row_count = count_lat * local_len
    head_dim = width // HEADS
    my_index = lax.axis_index("group")
    gathered = (
        lax.all_gather(qkv_weight, "group", axis=0, tiled=True),
        lax.all_gather(output_weight, "group", axis=0, tiled=True),
        lax.all_gather(up_weight, "group", axis=0, tiled=True),
        lax.all_gather(down_weight, "group", axis=0, tiled=True),
        lax.all_gather(query_bias, "group", axis=0, tiled=True),
        lax.all_gather(value_bias, "group", axis=0, tiled=True),
        lax.all_gather(output_bias, "group", axis=0, tiled=True),
        lax.all_gather(up_bias, "group", axis=0, tiled=True),
        lax.all_gather(down_bias, "group", axis=0, tiled=True),
        lax.all_gather(ada_bias, "group", axis=0, tiled=True),
    )
    (
        qkv_full,
        output_full,
        up_full,
        down_full,
        query_full,
        value_full,
        outbias_full,
        upbias_full,
        downbias_full,
        adabias_full,
    ) = gathered
    cond_float = cond.astype(jnp.float32)
    silu_cond, silu_back = jax.vjp(jax.nn.silu, cond_float)
    silu_low = silu_cond.astype(jnp.bfloat16)
    shard_rows = ada_weight.shape[0]
    silu_mine = lax.dynamic_slice_in_dim(silu_low, my_index * shard_rows, shard_rows, 1)
    partial_mod = jnp.dot(silu_mine, ada_weight, preferred_element_type=jnp.float32)
    modulation = lax.psum(partial_mod, "group") + adabias_full.astype(jnp.float32)
    parts = [modulation[:, None, index * width : (index + 1) * width] for index in range(6)]
    shift_one, scale_one, gate_one, shift_two, scale_two, gate_two = parts
    latent_float = latents.astype(jnp.float32)
    normed_one, inverse_one = norm_rows(latent_float)
    attn_in = (normed_one * (1.0 + scale_one) + shift_one).astype(jnp.bfloat16)
    attn_flat = attn_in.reshape(row_count, width)
    projected = jnp.dot(attn_flat, qkv_full, preferred_element_type=jnp.float32)
    queries = (
        (projected[:, :width] + query_full.astype(jnp.float32))
        .astype(jnp.bfloat16)
        .reshape(count_lat, local_len, width)
    )
    key_rows = (
        projected[:, width : 2 * width].astype(jnp.bfloat16).reshape(count_lat, local_len, width)
    )
    value_rows = (
        (projected[:, 2 * width :] + value_full.astype(jnp.float32))
        .astype(jnp.bfloat16)
        .reshape(count_lat, local_len, width)
    )
    group_count = lax.axis_size("group")
    both = jnp.concatenate([key_rows, value_rows], axis=2)
    both_whole = jnp.concatenate(
        [both] + [turn(both, "group", shift) for shift in range(1, group_count)], axis=1
    )
    key_whole, value_whole = both_whole[:, :, :width], both_whole[:, :, width:]
    mixed_low = jnp.concatenate(
        [
            attention(queries[index], key_whole[index], value_whole[index], head_dim)
            for index in range(count_lat)
        ],
        axis=0,
    )
    branch_one = (
        jnp.dot(mixed_low, output_full, preferred_element_type=jnp.float32)
        + outbias_full.astype(jnp.float32)
    ).reshape(count_lat, local_len, width)
    middle = latent_float + gate_one * branch_one
    normed_two, inverse_two = norm_rows(middle)
    mlp_in = (
        (normed_two * (1.0 + scale_two) + shift_two).astype(jnp.bfloat16).reshape(row_count, width)
    )
    hidden = jnp.dot(mlp_in, up_full, preferred_element_type=jnp.float32) + upbias_full.astype(
        jnp.float32
    )
    active, gelu_back = jax.vjp(lambda values: jax.nn.gelu(values, approximate=True), hidden)
    active_low = active.astype(jnp.bfloat16)
    branch_two = (
        jnp.dot(active_low, down_full, preferred_element_type=jnp.float32)
        + downbias_full.astype(jnp.float32)
    ).reshape(count_lat, local_len, width)
    block_out = (middle + gate_two * branch_two).astype(jnp.bfloat16)
    grad_out = cotangent.astype(jnp.float32)
    grad_gate_two = token_sum(grad_out * branch_two)
    grad_branch_two = (grad_out * gate_two).reshape(row_count, width)
    down_bias_term = jnp.sum(grad_branch_two, axis=0)
    branch_two_low = grad_branch_two.astype(jnp.bfloat16)
    down_share = group_rows(active_low, branch_two_low, down_weight.shape[0])
    grad_active = jnp.dot(branch_two_low, down_full.T, preferred_element_type=jnp.float32).astype(
        jnp.bfloat16
    )
    grad_hidden = gelu_back(grad_active.astype(jnp.float32))[0]
    up_bias_term = jnp.sum(grad_hidden, axis=0)
    hidden_low = grad_hidden.astype(jnp.bfloat16)
    up_share = group_rows(mlp_in, hidden_low, up_weight.shape[0])
    down_sum, up_sum = lax.psum((down_share, up_share), "replica")
    grad_mlp_in = jnp.dot(hidden_low, up_full.T, preferred_element_type=jnp.float32).reshape(
        count_lat, local_len, width
    )
    grad_shift_two = token_sum(grad_mlp_in)
    grad_scale_two = token_sum(grad_mlp_in * normed_two)
    grad_middle = grad_out + norm_back(normed_two, inverse_two, grad_mlp_in * (1.0 + scale_two))
    grad_gate_one = token_sum(grad_middle * branch_one)
    grad_branch_one = (grad_middle * gate_one).reshape(row_count, width)
    output_bias_term = jnp.sum(grad_branch_one, axis=0)
    branch_one_low = grad_branch_one.astype(jnp.bfloat16)
    output_share = group_rows(mixed_low, branch_one_low, output_weight.shape[0])
    grad_mixed = (
        jnp.dot(branch_one_low, output_full.T, preferred_element_type=jnp.float32)
        .astype(jnp.bfloat16)
        .reshape(count_lat, local_len, width)
    )

    grad_mixed = after(grad_mixed, up_share)
    pieces = [
        attention_back(
            queries[index], key_whole[index], value_whole[index], grad_mixed[index], head_dim
        )
        for index in range(count_lat)
    ]
    grad_query, key_terms, value_terms = [jnp.stack(items) for items in zip(*pieces)]
    grad_key, grad_value = key_terms[:, :local_len], value_terms[:, :local_len]
    for shift in range(1, group_count):
        block = slice(shift * local_len, (shift + 1) * local_len)
        grad_key = grad_key + turn(key_terms[:, block], "group", -shift)
        grad_value = grad_value + turn(value_terms[:, block], "group", -shift)
    query_low = grad_query.astype(jnp.bfloat16).reshape(row_count, width)
    key_low = grad_key.astype(jnp.bfloat16).reshape(row_count, width)
    value_low = grad_value.astype(jnp.bfloat16).reshape(row_count, width)
    query_bias_term = jnp.sum(query_low.astype(jnp.float32), axis=0)
    value_bias_term = jnp.sum(value_low.astype(jnp.float32), axis=0)
    grad_qkv = jnp.concatenate([query_low, key_low, value_low], axis=1)
    qkv_share = group_rows(attn_flat, grad_qkv, qkv_weight.shape[0])
    late_sum = replica_sum(jnp.concatenate([output_share, qkv_share], axis=1))
    output_sum, qkv_sum = late_sum[:, :width], late_sum[:, width:]
    grad_attn_in = jnp.dot(grad_qkv, qkv_full.T, preferred_element_type=jnp.float32).reshape(
        count_lat, local_len, width
    )
    grad_shift_one = token_sum(grad_attn_in)
    grad_scale_one = token_sum(grad_attn_in * normed_one)
    latents_grad = grad_middle + norm_back(
        normed_one, inverse_one, grad_attn_in * (1.0 + scale_one)
    )
    mod_terms = jnp.concatenate(
        [
            grad_shift_one,
            grad_scale_one,
            grad_gate_one,
            grad_shift_two,
            grad_scale_two,
            grad_gate_two,
        ],
        axis=1,
    )
    bias_terms = (
        query_bias_term,
        value_bias_term,
        output_bias_term,
        up_bias_term,
        down_bias_term,
    )
    bias_rows_all = jnp.concatenate(
        [term.reshape(group_count, -1) for term in bias_terms], axis=1
    )
    bias_share = lax.psum_scatter(bias_rows_all, "group", scatter_dimension=0, tiled=True)
    share_len = bias_share.shape[1]
    bias_spread = jnp.concatenate(
        [bias_share, jnp.zeros((count_lat - 1, share_len), jnp.float32)], axis=0
    )
    small = jnp.concatenate([mod_terms, silu_mine.astype(jnp.float32), bias_spread], axis=1)
    every = lax.all_gather(small, ("replica", "group"), axis=0).reshape(
        -1, group_count, count_lat, small.shape[1]
    )
    mod_every = jnp.sum(every[..., : 6 * width], axis=1).reshape(-1, 6 * width)
    mine_every = lax.dynamic_index_in_dim(every, my_index, 1, keepdims=False)
    mine_every = mine_every[..., 6 * width :].reshape(-1, shard_rows + share_len)
    silu_every = mine_every[:, :shard_rows].astype(jnp.bfloat16)
    bias_sum = jnp.sum(mine_every[:, shard_rows:], axis=0)
    grad_mod_low = mod_every.astype(jnp.bfloat16)
    bias_rows = ada_bias.shape[0]
    ada_bias_grad = lax.dynamic_slice_in_dim(
        jnp.sum(mod_every, axis=0), my_index * bias_rows, bias_rows, 0
    )
    ada_weight_grad = jnp.dot(silu_every.T, grad_mod_low, preferred_element_type=jnp.float32)
    grad_mod_mine = lax.dynamic_slice_in_dim(
        grad_mod_low, lax.axis_index("replica") * count_lat, count_lat, 0
    )
    silu_piece = jnp.dot(grad_mod_mine, ada_weight.T, preferred_element_type=jnp.float32)
    silu_grad = lax.all_gather(silu_piece, "group", axis=1, tiled=True)
    cond_grad = silu_back(silu_grad)[0]
    cuts, at = [], 0
    for term in bias_terms:
        cuts.append(bias_sum[at : at + term.shape[0] // group_count])
        at += term.shape[0] // group_count
    query_bias_grad, value_bias_grad, output_bias_grad, up_bias_grad, down_bias_grad = cuts
    return (
        block_out,
        latents_grad,
        cond_grad,
        ada_weight_grad,
        ada_bias_grad,
        qkv_sum.astype(jnp.float32),
        query_bias_grad,
        value_bias_grad,
        output_sum.astype(jnp.float32),
        output_bias_grad,
        up_sum.astype(jnp.float32),
        up_bias_grad,
        down_sum.astype(jnp.float32),
        down_bias_grad,
    )


def solution(mesh):
    return jax.shard_map(
        per_device,
        mesh=mesh,
        in_specs=(
            P("replica", "group", None),
            P("replica", None),
            P("replica", "group", None),
            P("group", None),
            P("group"),
            P("group", None),
            P("group"),
            P("group"),
            P("group", None),
            P("group"),
            P("group", None),
            P("group"),
            P("group", None),
            P("group"),
        ),
        out_specs=(
            P("replica", "group", None),
            P("replica", "group", None),
            P("replica", None),
            P("group", None),
            P("group"),
            P("group", None),
            P("group"),
            P("group"),
            P("group", None),
            P("group"),
            P("group", None),
            P("group"),
            P("group", None),
            P("group"),
        ),
        check_vma=False,
    )
```

time: 887 us -> 614 us (0.69)
  waiting for transfers between devices: 439 us -> 310 us
  matrix products: 208 us -> 107 us
  blocking collectives: 106 us -> 22.9 us
  Pallas kernels: 0 us -> 60.3 us
  other arithmetic: 89.4 us -> 55.6 us
  starting transfers between devices: 1.16 us -> 15.7 us
    psum x1, waiting for transfers between devices: 417 us -> 156 us  [per_device(): down_sum, up_sum = lax.psum((down_share, up_share), 'replica')]
    ppermute x0 -> x23, waiting for transfers between devices: none -> 133 us  [the longest x8 94 us: pair_sum(): away = lax.ppermute(jnp.where(upper, low, high), 'replica', pair)]
    dot_general x15 -> x14, matrix products: 170 us -> 67.9 us  [the longest x8 32.7 us: term(): return jnp.dot(part.T, right, preferred_element_type=jnp.float32)]
    psum x2 -> x0, blocking collectives: 85.6 us -> none  [the longest x1 81.4 us: per_device(): lax.psum(ada_bias_term.astype(jnp.bfloat16), 'replica').astype(jnp.float32)]
    pallas_call x0 -> x2, Pallas kernels: none -> 60.3 us  [the longest x1 36.4 us: attention_back(): pl.pallas_call(functools.partial(attend_back_kernel, head_dim), grid=(wid...]
    convert_element_type x14 -> x8, other arithmetic: 63.9 us -> 17.4 us  [the longest x1 6.82 us: per_device(): up_sum.astype(jnp.float32)]
    ppermute x0 -> x23, starting transfers between devices: none -> 15.3 us  [the longest x8 6.84 us: pair_sum(): away = lax.ppermute(values, 'replica', pair)]
    all_gather x2 -> x1, waiting for transfers between devices: 0.02 us -> 13.8 us  [per_device(): lax.all_gather(small, ('replica', 'group'), axis=0)]
  transfers between devices with their start and end apart: 13 -> 29, of which waited for: 3 -> 13; matrix products, arithmetic and copies ran while one was open for 25% -> 23% of each run, Pallas kernels for 0% -> 4%
where the time goes in v1:
time: 614 us; the launch traced here: 609 us
  waiting for transfers between devices  310 us (50%)
  matrix products  107 us (17%)
  Pallas kernels  60.3 us (10%)
  other arithmetic  55.6 us (9%)
  blocking collectives  22.9 us (4%)
  local copies, waits for them, and re-layouts  21.8 us (4%)
  starting transfers between devices  15.7 us (3%)
  between operations  15.5 us (3%)
    psum x1, waiting for transfers between devices, per_device(): down_sum, up_sum = lax.psum((down_share, up_share), 'replica')  156 us
    ppermute x8, waiting for transfers between devices, pair_sum(): away = lax.ppermute(jnp.where(upper, low, high), 'replica', pair)  94 us
    ppermute x8, waiting for transfers between devices, pair_sum(): away = lax.ppermute(values, 'replica', pair)  38.9 us
    pallas_call x1, Pallas kernels, attention_back(): pl.pallas_call(functools.partial(attend_back_kernel, head_dim), grid=(wid...  36.4 us
    dot_general x8, matrix products, term(): return jnp.dot(part.T, right, preferred_element_type=jnp.float32)  32.7 us
    pallas_call x1, Pallas kernels, attention(): pl.pallas_call(functools.partial(attend_kernel, head_dim), grid=(width //...  23.9 us
    all_gather x1, waiting for transfers between devices, per_device(): lax.all_gather(small, ('replica', 'group'), axis=0)  13.8 us
    dot_general x1, matrix products, per_device(): jnp.dot(branch_two_low, down_full.T, preferred_element_type=jnp.float32)  13.6 us
  transfers between devices with their start and end apart: 29, of which 13 were waited for; matrix products, arithmetic and copies ran while one was open for 23% of the time, Pallas kernels for 4%

profile of v1, /device:TPU:0, one launch (start us, length us, event | category | flops | bytes accessed | tf_op | source)
XLA Modules:
  0.0 608.8 jit_solution(15570909129386740291)
XLA Ops:
  10.2 3.8 fusion.90
  14.0 3.8 psum.21
  24.4 4.6 all-gather.14.cloned.1.call-done
  29.1 5.5 fusion.50
  37.2 3.9 all-gather.5
  45.0 9.1 %pad_maximum_fusion = bf16[1,1024,2048]{2,1,0:T(8,128)(2,1)S(1)} fusion(bf16[1,512,2048]{2,1,0:T(8,128)(2,1)} %collective-permute-done, bf16[1,512,1024]{2,1,0:T(8,128)(2,1)S(1)} %get-tuple-element.46, bf16[1,512,1024]{2,1,0:T(8,128)(2,1)S(1)} %fusion.43), kind=kLoop, calls=%fused_computation.20 | loop fusion | flops 12582912 | bytes 8388608 | tf_op jit(solution)/shard_map/concatenate | solution.py:262
  55.9 23.9 %attend.1 = bf16[512,1024]{1,0:T(8,128)(2,1)S(1)} custom-call(bf16[512,1024]{1,0:T(8,128)(2,1)S(1)} %get-tuple-element.47.query_ref, bf16[1024,1024]{1,0:T(8,128)(2,1)S(1)} %get-tuple-element.49.key_ref, bf16[1024,1024]{1,0:T(8,128)(2,1)} %get-tuple-element.48.value_ref), custom_call_target="tpu_custom_call" | custom-call | flops 8589934592 | bytes 6291456 | tf_op jit(solution)/shard_map/attend/pallas_call | solution.py:92
  80.8 5.6 fusion.100
  88.1 12.7 %multiply_convert_fusion = (bf16[512,4096]{1,0:T(8,128)(2,1)}, f32[512,4096]{1,0:T(8,128)}) fusion(f32[4096]{0:T(1024)S(1)} %convert_element_type.148, bf16[1024,4096]{1,0:T(8,128)(2,1)} %all-gather.18.cloned.1.call-done, bf16[1,512,1024]{2,1,0:T(8,128)(2,1)S(1)} %add_convert_fusion.4), kind=kOutput, calls=%fused_computation.15 | convolution fusion | flops 4315938816 | bytes 22036480 | tf_op jit(solution)/shard_map/dot_general | solution.py:282
  100.8 13.6 %fusion.103 = (f32[4096]{0:T(1024)S(1)}, bf16[512,4096]{1,0:T(8,128)(2,1)S(1)}) fusion(f32[512,4096]{1,0:T(8,128)} %get-tuple-element.67, f32[4096]{0:T(1024)S(1)} %convert_element_type.148, bf16[4096,1024]{1,0:T(8,128)(2,1)} %all-gather.20.cloned.1.call-done, bf16[1,512,1024]{2,1,0:T(8,128)(2,1)} %param.16, f32[1024]{0:T(1024)S(1)} %bitcast.172), kind=kOutput, calls=%fused_computation.198 | convolution fusion | flops 4346867712 | bytes 22056960 | tf_op jit(solution)/shard_map/dot_general | solution.py:298
  117.1 8.3 %fusion.31 = (f32[1024]{0:T(1024)S(1)}, f32[512]{0:T(512)S(1)}, f32[512,1024]{1,0:T(8,128)S(1)}) fusion(f32[1,512,1024]{2,1,0:T(8,128)S(1)} %copy-done.9, f32[512]{0:T(512)S(1)} %add_rsqrt_fusion, f32[512]{0:T(512)S(1)} %broadcast_multiply_fusion.4, f32[1024]{0:T(1024)S(1)} %bitcast.159, bf16[1024,4096]{1,0:T(8,128)(2,1)} %all-gather.18.cloned.1.call-done, ...), kind=kOutput, calls=%fused_computation.63 | convolution fusion | flops 4298635776 | bytes 16791552 | tf_op jit(solution)/shard_map/dot_general | solution.py:306
  126.6 11.7 %fusion.16 = (f32[1024]{0:T(1024)S(1)}, f32[1024]{0:T(1024)S(1)}, bf16[1,512,1024]{2,1,0:T(8,128)(2,1)}, f32[1024]{0:T(1024)S(1)}, f32[1024]{0:T(1024)S(1)}, /*index=5*/f32[1,512,1024]{2,1,0:T(8,128)S(1)}) fusion(bf16[1,512,1024]{2,1,0:T(8,128)(2,1)S(1)} %copy-done.37, f32[1024]{0:T(1024)S(1)} %bitcast.173, f32[1024]{0:T(1024)S(1)} %bitcast.179, ...), kind=kOutput, calls=%fused_computation.37 | convolution fusion | flops 4306497536 | bytes 23113728 | tf_op jit(solution)/shard_map/dot_general | solution.py:288
  142.3 4.4 add_convert_fusion.1
  146.8 36.4 %attend_back.1 = (bf16[512,1024]{1,0:T(8,128)(2,1)S(1)}, f32[1024,1024]{1,0:T(8,128)}, f32[1024,1024]{1,0:T(8,128)}) custom-call(bf16[512,1024]{1,0:T(8,128)(2,1)S(1)} %copy-done.1, bf16[1024,1024]{1,0:T(8,128)(2,1)S(1)} %get-tuple-element.49.key_ref, bf16[1024,1024]{1,0:T(8,128)(2,1)} %get-tuple-element.48.value_ref, bf16[512,1024]{1,0:T(8,128)(2,1)S(1)} %bitcast.141), custom_call_target="tpu_custom_call" | custom-call | flops 21474836480 | bytes 20971520 | tf_op jit(solution)/shard_map/attend_back/pallas_call | solution.py:114
  191.3 6.0 convolution_convert_fusion.3
  201.4 3.9 all-reduce
  222.7 4.2 add_convert_fusion.2
  231.4 6.7 %add_convert_fusion = bf16[2048,1024]{1,0:T(8,128)(2,1)} fusion(bf16[2048,1024]{1,0:T(8,128)(2,1)} %collective-permute-done.22, bf16[512,4096]{1,0:T(8,128)(2,1)S(1)} %copy-done.41, s32[]{:T(128)S(6)} %select_n.206, bf16[1,512,1024]{2,1,0:T(8,128)(2,1)S(1)} %copy-done.39, f32[1024]{0:T(1024)S(1)} %bitcast.175), kind=kOutput, calls=%fused_computation.13 | convolution fusion | flops 2155347968 | bytes 11538436 | tf_op jit(solution)/shard_map/dot_general | solution.py:144
  243.5 12.6 %collective-permute-done.14 = bf16[256,2048]{1,0:T(8,128)(2,1)} collective-permute-done((bf16[256,2048]{1,0:T(8,128)(2,1)}, bf16[256,2048]{1,0:T(8,128)(2,1)}, u32[]{:S(2)}, u32[]{:S(2)}) %collective-permute-start.14) | collective-permute-done | bytes 1048608 | tf_op jit(solution)/shard_map/ppermute | solution.py:163
  262.4 13.8 %all-gather.22.cloned.1.call-done = f32[32,1,10752]{2,1,0:T(1,128)} async-done(((f32[1,1,10752]{2,1,0:T(1,128)}), f32[32,1,10752]{2,1,0:T(1,128)}) %all-gather.22.cloned.1.call-update) | async-done | bytes 1376272 | tf_op jit(solution)/shard_map/all_gather | solution.py:380
  281.9 32.4 %collective-permute-done.6 = bf16[256,2048]{1,0:T(8,128)(2,1)S(1)} collective-permute-done((bf16[256,2048]{1,0:T(8,128)(2,1)}, bf16[256,2048]{1,0:T(8,128)(2,1)S(1)}, u32[]{:S(2)}, u32[]{:S(2)}) %collective-permute-start.6) | collective-permute-done | bytes 1048608 | tf_op jit(solution)/shard_map/ppermute | solution.py:163
  316.8 11.5 %collective-permute-done.7 = bf16[128,2048]{1,0:T(8,128)(2,1)S(1)} collective-permute-done((bf16[128,2048]{1,0:T(8,128)(2,1)S(1)}, bf16[128,2048]{1,0:T(8,128)(2,1)S(1)}, u32[]{:S(2)}, u32[]{:S(2)}) %collective-permute-start.7) | collective-permute-done | bytes 524320 | tf_op jit(solution)/shard_map/ppermute | solution.py:163
  328.6 4.1 collective-permute-done.17
  332.9 22.5 %collective-permute-done.8 = bf16[64,2048]{1,0:T(8,128)(2,1)S(1)} collective-permute-done((bf16[64,2048]{1,0:T(8,128)(2,1)S(1)}, bf16[64,2048]{1,0:T(8,128)(2,1)S(1)}, u32[]{:S(2)}, u32[]{:S(2)}) %collective-permute-start.8) | collective-permute-done | bytes 262176 | tf_op jit(solution)/shard_map/ppermute | solution.py:163
  358.6 10.9 %collective-permute-done.9 = bf16[32,2048]{1,0:T(8,128)(2,1)S(1)} collective-permute-done((bf16[32,2048]{1,0:T(8,128)(2,1)S(1)}, bf16[32,2048]{1,0:T(8,128)(2,1)S(1)}, u32[]{:S(2)}, u32[]{:S(2)}) %collective-permute-start.9) | collective-permute-done | bytes 131104 | tf_op jit(solution)/shard_map/ppermute | solution.py:163
  369.6 13.0 %collective-permute-done.19 = bf16[64,2048]{1,0:T(8,128)(2,1)S(1)} collective-permute-done((bf16[64,2048]{1,0:T(8,128)(2,1)S(1)}, bf16[64,2048]{1,0:T(8,128)(2,1)S(1)}, u32[]{:S(2)}, u32[]{:S(2)}) %collective-permute-start.19) | collective-permute-done | bytes 262176 | tf_op jit(solution)/shard_map/ppermute | solution.py:167
  387.7 4.5 collective-permute-done.11
  398.7 19.0 %collective-permute-done.12 = bf16[128,2048]{1,0:T(8,128)(2,1)S(1)} collective-permute-done((bf16[128,2048]{1,0:T(8,128)(2,1)S(1)}, bf16[128,2048]{1,0:T(8,128)(2,1)S(1)}, u32[]{:S(2)}, u32[]{:S(2)}) %collective-permute-start.12) | collective-permute-done | bytes 524320 | tf_op jit(solution)/shard_map/ppermute | solution.py:167
  419.3 6.6 %fusion.76 = f32[512,6144]{1,0:T(8,128)} fusion(bf16[16,6144]{1,0:T(8,128)(2,1)S(1)} %get-tuple-element.33, f32[16,4608]{1,0:T(8,128)S(1)} %bitcast.151), kind=kOutput, calls=%fused_computation.158 | convolution fusion | flops 100663296 | bytes 12795904 | tf_op jit(solution)/shard_map/dot_general | solution.py:393
  425.9 155.9 %all-reduce.4.cloned.1.call-done = (bf16[512,4096]{1,0:T(8,128)(2,1)}, bf16[2048,1024]{1,0:T(8,128)(2,1)}) async-done(((bf16[512,4096]{1,0:T(8,128)(2,1)}, bf16[2048,1024]{1,0:T(8,128)(2,1)}), (bf16[512,4096]{1,0:T(8,128)(2,1)}, bf16[2048,1024]{1,0:T(8,128)(2,1)})) %all-reduce.4.cloned.1.call-update) | async-done | bytes 8388624 | tf_op jit(solution)/shard_map/psum | solution.py:305
  581.8 6.8 %convert_element_type.178 = f32[512,4096]{1,0:T(8,128)} convert(bf16[512,4096]{1,0:T(8,128)(2,1)} %get-tuple-element.36) | non-fusion elementwise | flops 2097152 | bytes 12582912 | tf_op jit(solution)/shard_map/convert_element_type | solution.py:416
  588.6 4.4 convert_element_type.182
  (252 shorter events, 107.1 us)
Async XLA Ops:
  7.2 21.9 %all-gather.14.cloned.1.call-start = ((), (), s32[]{:S(2)}) async-start(), calls=%async_computation | async-start | bytes 9437184 | tf_op jit(solution)/shard_map/all_gather | solution.py:210
  7.9 72.9 %all-gather.16.cloned.1.call-start = ((), (), s32[]{:S(2)}) async-start(), calls=%async_computation.1 | async-start | bytes 3145728 | tf_op jit(solution)/shard_map/all_gather | solution.py:211
  8.7 79.5 %all-gather.18.cloned.1.call-start = ((), (), s32[]{:S(2)}) async-start(), calls=%async_computation.2 | async-start | bytes 12582912 | tf_op jit(solution)/shard_map/all_gather | solution.py:212
  9.4 91.4 %all-gather.20.cloned.1.call-start = ((), (), s32[]{:S(2)}) async-start(), calls=%async_computation.3 | async-start | bytes 12582912 | tf_op jit(solution)/shard_map/all_gather | solution.py:213
  10.0 266.2 %all-gather.22.cloned.1.call-start = ((), (), s32[]{:S(2)}) async-start(), calls=%async_computation.4 | async-start | bytes 1419264 | tf_op jit(solution)/shard_map/all_gather | solution.py:380
  37.0 8.0 %collective-permute-start = (bf16[1,512,2048]{2,1,0:T(8,128)(2,1)}, bf16[1,512,2048]{2,1,0:T(8,128)(2,1)}, u32[]{:S(2)}, u32[]{:S(2)}) collective-permute-start(bf16[1,512,2048]{2,1,0:T(8,128)(2,1)} %pad_maximum_fusion.3), channel_id=1, source_target_pairs={{0,16},{16,0},{1,17},{17,1},{2,18},{18,2},{3,19},{19,3},{4,20},{20... | collective-permute-start | bytes 6291464 | tf_op jit(solution)/shard_map/ppermute | solution.py:136
  116.9 25.4 %collective-permute-start.1 = (bf16[512,4096]{1,0:T(8,128)(2,1)S(1)}, bf16[512,4096]{1,0:T(8,128)(2,1)S(1)}, u32[]{:S(2)}, u32[]{:S(2)}) collective-permute-start(bf16[512,4096]{1,0:T(8,128)(2,1)S(1)} %convolution_convert_fusion.1), channel_id=1, source_target_pairs={{0,16},{16,0},{1,17},{17,1},{2,18},{18,2},{3,19},{19,3},{4,20},{20... | collective-permute-start | bytes 12582920 | tf_op jit(solution)/shard_map/ppermute | solution.py:136
  186.5 11.2 %collective-permute-start.3 = (f32[1,512,1024]{2,1,0:T(8,128)}, f32[1,512,1024]{2,1,0:T(8,128)}, u32[]{:S(2)}, u32[]{:S(2)}) collective-permute-start(f32[1,512,1024]{2,1,0:T(8,128)} %slice.190), channel_id=1, source_target_pairs={{0,16},{16,0},{1,17},{17,1},{2,18},{18,2},{3,19},{19,3},{4,20},{20... | collective-permute-start | bytes 6291464 | tf_op jit(solution)/shard_map/ppermute | solution.py:136
  188.3 17.1 %collective-permute-start.2 = (f32[1,512,1024]{2,1,0:T(8,128)}, f32[1,512,1024]{2,1,0:T(8,128)}, u32[]{:S(2)}, u32[]{:S(2)}) collective-permute-start(f32[1,512,1024]{2,1,0:T(8,128)} %slice.188), channel_id=1, source_target_pairs={{0,16},{16,0},{1,17},{17,1},{2,18},{18,2},{3,19},{19,3},{4,20},{20... | collective-permute-start | bytes 6291464 | tf_op jit(solution)/shard_map/ppermute | solution.py:136
  191.0 28.2 %collective-permute-start.4 = (bf16[512,1024]{1,0:T(8,128)(2,1)}, bf16[512,1024]{1,0:T(8,128)(2,1)}, u32[]{:S(2)}, u32[]{:S(2)}) collective-permute-start(bf16[512,1024]{1,0:T(8,128)(2,1)} %convolution_convert_fusion.5), channel_id=1, source_target_pairs={{0,16},{16,0},{1,17},{17,1},{2,18},{18,2},{3,19},{19,3},{4,20},{20... | collective-permute-start | bytes 3145736 | tf_op jit(solution)/shard_map/ppermute | solution.py:136
  197.3 34.1 %collective-permute-start.22 = (bf16[2048,1024]{1,0:T(8,128)(2,1)}, bf16[2048,1024]{1,0:T(8,128)(2,1)}, u32[]{:S(2)}, u32[]{:S(2)}) collective-permute-start(bf16[2048,1024]{1,0:T(8,128)(2,1)} %convolution_convert_fusion.3), channel_id=1, source_target_pairs={{0,16},{16,0},{1,17},{17,1},{2,18},{18,2},{3,19},{19,3},{4,20},{20... | collective-permute-start | bytes 12582920 | tf_op jit(solution)/shard_map/ppermute | solution.py:136
  211.8 10.9 %collective-permute-start.5 = (bf16[512,3072]{1,0:T(8,128)(2,1)}, bf16[512,3072]{1,0:T(8,128)(2,1)}, u32[]{:S(2)}, u32[]{:S(2)}) collective-permute-start(bf16[512,3072]{1,0:T(8,128)(2,1)} %convolution_convert_fusion.2), channel_id=1, source_target_pairs={{0,16},{16,0},{1,17},{17,1},{2,18},{18,2},{3,19},{19,3},{4,20},{20... | collective-permute-start | bytes 9437192 | tf_op jit(solution)/shard_map/ppermute | solution.py:136
  218.9 362.9 %all-reduce.4.cloned.1.call-start = ((), (), s32[]{:S(2)}) async-start(), calls=%async_computation.5 | async-start | bytes 16777216 | tf_op jit(solution)/shard_map/psum | solution.py:305
  229.7 26.4 %collective-permute-start.14 = (bf16[256,2048]{1,0:T(8,128)(2,1)}, bf16[256,2048]{1,0:T(8,128)(2,1)}, u32[]{:S(2)}, u32[]{:S(2)}) collective-permute-start(bf16[256,2048]{1,0:T(8,128)(2,1)} %broadcast_select_fusion.1), channel_id=1, source_target_pairs={{0,2},{1,3},{2,0},{3,1},{4,6},{5,7},{6,4},{7,5},{8,10},{9,11},{10,... | collective-permute-start | bytes 3145736 | tf_op jit(solution)/shard_map/ppermute | solution.py:163
  259.8 126.1 %slice-start = ((s8[6291456]{0:T(1024)(128)(4,1)}), s8[2097152]{0:T(1024)(128)(4,1)S(1)}, s32[]{:S(2)}) async-start(s8[6291456]{0:T(1024)(128)(4,1)} %bitcast.142), calls=%async_computation.6 | async-start | bytes 4194304
  260.6 19.5 %collective-permute-start.15 = (bf16[128,2048]{1,0:T(8,128)(2,1)}, bf16[128,2048]{1,0:T(8,128)(2,1)}, u32[]{:S(2)}, u32[]{:S(2)}) collective-permute-start(bf16[128,2048]{1,0:T(8,128)(2,1)} %broadcast_select_fusion.2), channel_id=1, source_target_pairs={{0,1},{1,0},{2,3},{3,2},{4,5},{5,4},{6,7},{7,6},{8,9},{9,8},{10,11... | collective-permute-start | bytes 1572872 | tf_op jit(solution)/shard_map/ppermute | solution.py:163
  277.3 37.0 %copy-start.14 = (bf16[256,2048]{1,0:T(8,128)(2,1)S(1)}, bf16[256,2048]{1,0:T(8,128)(2,1)}, u32[]{:S(2)}) copy-start(bf16[256,2048]{1,0:T(8,128)(2,1)} %get-tuple-element.39) | copy-start | bytes 3145732
  277.3 36.9 %collective-permute-start.6 = (bf16[256,2048]{1,0:T(8,128)(2,1)}, bf16[256,2048]{1,0:T(8,128)(2,1)S(1)}, u32[]{:S(2)}, u32[]{:S(2)}) collective-permute-start(bf16[256,2048]{1,0:T(8,128)(2,1)} %get-tuple-element.38), channel_id=1, source_target_pairs={{0,1},{1,0},{2,3},{3,2},{4,5},{5,4},{6,7},{7,6},{8,9},{9,8},{10,11... | collective-permute-start | bytes 3145736 | tf_op jit(solution)/shard_map/ppermute | solution.py:163
  281.3 34.8 %collective-permute-start.16 = (bf16[64,2048]{1,0:T(8,128)(2,1)S(1)}, bf16[64,2048]{1,0:T(8,128)(2,1)S(1)}, u32[]{:S(2)}, u32[]{:S(2)}) collective-permute-start(bf16[64,2048]{1,0:T(8,128)(2,1)S(1)} %broadcast_select_fusion.4), channel_id=1, source_target_pairs={{0,4},{1,5},{2,6},{3,7},{4,0},{5,1},{6,2},{7,3},{8,12},{9,13},{10,... | collective-permute-start | bytes 786440 | tf_op jit(solution)/shard_map/ppermute | solution.py:163
  314.3 71.6 %slice-start.1 = ((s8[6291456]{0:T(1024)(128)(4,1)}), s8[4194304]{0:T(1024)(128)(4,1)S(1)}, s32[]{:S(2)}) async-start(s8[6291456]{0:T(1024)(128)(4,1)} %bitcast.142), calls=%async_computation.7 | async-start | bytes 8388608
  314.5 13.9 %collective-permute-start.7 = (bf16[128,2048]{1,0:T(8,128)(2,1)S(1)}, bf16[128,2048]{1,0:T(8,128)(2,1)S(1)}, u32[]{:S(2)}, u32[]{:S(2)}) collective-permute-start(bf16[128,2048]{1,0:T(8,128)(2,1)S(1)} %broadcast_select_fusion.3), channel_id=1, source_target_pairs={{0,2},{1,3},{2,0},{3,1},{4,6},{5,7},{6,4},{7,5},{8,10},{9,11},{10,... | collective-permute-start | bytes 1572872 | tf_op jit(solution)/shard_map/ppermute | solution.py:163
  316.2 16.6 %collective-permute-start.17 = (bf16[32,2048]{1,0:T(8,128)(2,1)S(1)}, bf16[32,2048]{1,0:T(8,128)(2,1)S(1)}, u32[]{:S(2)}, u32[]{:S(2)}) collective-permute-start(bf16[32,2048]{1,0:T(8,128)(2,1)S(1)} %broadcast_select_fusion.6), channel_id=1, source_target_pairs={{0,8},{1,9},{2,10},{3,11},{4,12},{5,13},{6,14},{7,15},{8,0},{9,1},... | collective-permute-start | bytes 393224 | tf_op jit(solution)/shard_map/ppermute | solution.py:163
  328.5 26.9 %collective-permute-start.8 = (bf16[64,2048]{1,0:T(8,128)(2,1)S(1)}, bf16[64,2048]{1,0:T(8,128)(2,1)S(1)}, u32[]{:S(2)}, u32[]{:S(2)}) collective-permute-start(bf16[64,2048]{1,0:T(8,128)(2,1)S(1)} %broadcast_select_fusion.5), channel_id=1, source_target_pairs={{0,4},{1,5},{2,6},{3,7},{4,0},{5,1},{6,2},{7,3},{8,12},{9,13},{10,... | collective-permute-start | bytes 786440 | tf_op jit(solution)/shard_map/ppermute | solution.py:163
  332.8 22.8 %collective-permute-start.18 = (bf16[32,2048]{1,0:T(8,128)(2,1)S(1)}, bf16[32,2048]{1,0:T(8,128)(2,1)S(1)}, u32[]{:S(2)}, u32[]{:S(2)}) collective-permute-start(bf16[32,2048]{1,0:T(8,128)(2,1)S(1)} %select_add_fusion.6), channel_id=1, source_target_pairs={{0,8},{1,9},{2,10},{3,11},{4,12},{5,13},{6,14},{7,15},{8,0},{9,1},... | collective-permute-start | bytes 393224 | tf_op jit(solution)/shard_map/ppermute | solution.py:167
  355.5 14.0 %collective-permute-start.9 = (bf16[32,2048]{1,0:T(8,128)(2,1)S(1)}, bf16[32,2048]{1,0:T(8,128)(2,1)S(1)}, u32[]{:S(2)}, u32[]{:S(2)}) collective-permute-start(bf16[32,2048]{1,0:T(8,128)(2,1)S(1)} %broadcast_select_fusion.7), channel_id=1, source_target_pairs={{0,8},{1,9},{2,10},{3,11},{4,12},{5,13},{6,14},{7,15},{8,0},{9,1},... | collective-permute-start | bytes 393224 | tf_op jit(solution)/shard_map/ppermute | solution.py:163
  355.6 27.0 %collective-permute-start.19 = (bf16[64,2048]{1,0:T(8,128)(2,1)S(1)}, bf16[64,2048]{1,0:T(8,128)(2,1)S(1)}, u32[]{:S(2)}, u32[]{:S(2)}) collective-permute-start(bf16[64,2048]{1,0:T(8,128)(2,1)S(1)} %maximum_select_fusion.7), channel_id=1, source_target_pairs={{0,4},{1,5},{2,6},{3,7},{4,0},{5,1},{6,2},{7,3},{8,12},{9,13},{10,... | collective-permute-start | bytes 786440 | tf_op jit(solution)/shard_map/ppermute | solution.py:167
  369.5 16.2 %collective-permute-start.10 = (bf16[32,2048]{1,0:T(8,128)(2,1)S(1)}, bf16[32,2048]{1,0:T(8,128)(2,1)S(1)}, u32[]{:S(2)}, u32[]{:S(2)}) collective-permute-start(bf16[32,2048]{1,0:T(8,128)(2,1)S(1)} %select_add_fusion.7), channel_id=1, source_target_pairs={{0,8},{1,9},{2,10},{3,11},{4,12},{5,13},{6,14},{7,15},{8,0},{9,1},... | collective-permute-start | bytes 393224 | tf_op jit(solution)/shard_map/ppermute | solution.py:167
  382.7 11.2 %collective-permute-start.20 = (bf16[128,2048]{1,0:T(8,128)(2,1)S(1)}, bf16[128,2048]{1,0:T(8,128)(2,1)S(1)}, u32[]{:S(2)}, u32[]{:S(2)}) collective-permute-start(bf16[128,2048]{1,0:T(8,128)(2,1)S(1)} %maximum_select_fusion.5), channel_id=1, source_target_pairs={{0,1},{1,0},{2,3},{3,2},{4,5},{5,4},{6,7},{7,6},{8,9},{9,8},{10,11... | collective-permute-start | bytes 1572872 | tf_op jit(solution)/shard_map/ppermute | solution.py:167
  385.8 6.4 %collective-permute-start.11 = (bf16[64,2048]{1,0:T(8,128)(2,1)S(1)}, bf16[64,2048]{1,0:T(8,128)(2,1)S(1)}, u32[]{:S(2)}, u32[]{:S(2)}) collective-permute-start(bf16[64,2048]{1,0:T(8,128)(2,1)S(1)} %maximum_select_fusion.6), channel_id=1, source_target_pairs={{0,4},{1,5},{2,6},{3,7},{4,0},{5,1},{6,2},{7,3},{8,12},{9,13},{10,... | collective-permute-start | bytes 786440 | tf_op jit(solution)/shard_map/ppermute | solution.py:167
  392.3 25.3 %collective-permute-start.12 = (bf16[128,2048]{1,0:T(8,128)(2,1)S(1)}, bf16[128,2048]{1,0:T(8,128)(2,1)S(1)}, u32[]{:S(2)}, u32[]{:S(2)}) collective-permute-start(bf16[128,2048]{1,0:T(8,128)(2,1)S(1)} %maximum_select_fusion.4), channel_id=1, source_target_pairs={{0,2},{1,3},{2,0},{3,1},{4,6},{5,7},{6,4},{7,5},{8,10},{9,11},{10,... | collective-permute-start | bytes 1572872 | tf_op jit(solution)/shard_map/ppermute | solution.py:167
  394.2 198.8 %collective-permute-start.21 = (bf16[256,2048]{1,0:T(8,128)(2,1)S(1)}, bf16[256,2048]{1,0:T(8,128)(2,1)S(1)}, u32[]{:S(2)}, u32[]{:S(2)}) collective-permute-start(bf16[256,2048]{1,0:T(8,128)(2,1)S(1)} %maximum_select_fusion.3), channel_id=1, source_target_pairs={{0,2},{1,3},{2,0},{3,1},{4,6},{5,7},{6,4},{7,5},{8,10},{9,11},{10,... | collective-permute-start | bytes 3145736 | tf_op jit(solution)/shard_map/ppermute | solution.py:167
  417.9 176.1 %collective-permute-start.13 = (bf16[256,2048]{1,0:T(8,128)(2,1)S(1)}, bf16[256,2048]{1,0:T(8,128)(2,1)}, u32[]{:S(2)}, u32[]{:S(2)}) collective-permute-start(bf16[256,2048]{1,0:T(8,128)(2,1)S(1)} %maximum_select_fusion.2), channel_id=1, source_target_pairs={{0,1},{1,0},{2,3},{3,2},{4,5},{5,4},{6,7},{7,6},{8,9},{9,8},{10,11... | collective-permute-start | bytes 3145736 | tf_op jit(solution)/shard_map/ppermute | solution.py:167
  (43 other events, 256.0 us)
Sparse Core Ops, SparseCore 0:
  9.6 19.4 all-gather.13
  30.6 12.1 all-gather.15
  44.4 21.0 all-gather.17
  66.8 21.0 all-gather.19
  219.0 57.1 all-gather.21
  282.8 298.9 all-reduce.3
